TPU v7x, 512 devices: a whole 4x4x16 slice. The times are simulated.
512 devices in a mesh: group: 8 (over x, core), dev: 64 (over z, y).
Axes of the slice: x: 4, y: 4, z: 16, core: 2. Of those that a mesh axis runs over, the one named last changes fastest.
Arguments:
- cam_jac: float32 [2, 9, 8, 262144], P(None, None, None, ('group', 'dev')), may hold values from -6 to 6
- lm_jac: float32 [2, 3, 8, 262144], P(None, None, None, ('group', 'dev')), may hold values from -6 to 6
- resid: float32 [2, 8, 262144], P(None, None, ('group', 'dev')), may hold values from -6 to 6
- cam_index: int32 [8, 262144], P(None, ('group', 'dev')), may hold values from 0 to 8191
Outputs:
- camera_step: float32 [9, 8192], P(None, 'dev')
- camera_residual: float32 [9, 8192], P(None, 'dev')
- landmark_step: float32 [3, 262144], P(None, ('group', 'dev'))
Inputs may be any that keep to these rules, and one draw needn't show every extreme that they name: `cam_index`: every observation names one of the 8192 cameras.
All inputs are finite; a program needn't handle non-finite values.
Results may differ from a plain program's by a relative error of at most 0.0003.
Values sent between devices are 32-bit elements; how exact they have to be, the bound alone decides.
A program may use at most 64 MiB of HBM per device.

v0:
```python
import jax
import jax.numpy as jnp
from jax import lax
from jax.sharding import PartitionSpec as P

CAM_DEV = 128
ITERS = 2
DAMPING = 1.0


def landmark_inverse(lm_jac):

    def entry(first, second):
        return jnp.sum(lm_jac[:, first] * lm_jac[:, second], axis=(0, 1))

    w_00 = entry(0, 0) + DAMPING
    w_11 = entry(1, 1) + DAMPING
    w_22 = entry(2, 2) + DAMPING
    w_01 = entry(0, 1)
    w_02 = entry(0, 2)
    w_12 = entry(1, 2)
    cof_00 = w_11 * w_22 - w_12 * w_12
    cof_01 = w_02 * w_12 - w_01 * w_22
    cof_02 = w_01 * w_12 - w_02 * w_11
    cof_11 = w_00 * w_22 - w_02 * w_02
    cof_12 = w_01 * w_02 - w_00 * w_12
    cof_22 = w_00 * w_11 - w_01 * w_01
    determinant = w_00 * cof_00 + w_01 * cof_01 + w_02 * cof_02
    rows = [
        jnp.stack([cof_00, cof_01, cof_02]),
        jnp.stack([cof_01, cof_11, cof_12]),
        jnp.stack([cof_02, cof_12, cof_22]),
    ]
    return jnp.stack(rows) / determinant[None, None]


def apply_inverse(inverse, vector):
    return jnp.sum(inverse * vector[None], axis=1)


def landmark_side(lm_jac, values):
    return jnp.sum(lm_jac * values[:, None], axis=(0, 2))


def back_project(lm_jac, landmark):
    return jnp.sum(lm_jac * landmark[None, :, None, :], axis=1)


def camera_apply(cam_jac, cam_values):
    return jnp.sum(cam_jac * cam_values[None], axis=1)


def camera_transpose(cam_jac, errors):
    return jnp.sum(cam_jac * errors[:, None], axis=0)


def to_cameras(values, cam_index, total_cams):
    flat_index = cam_index.reshape(-1)
    width = values.shape[0]

    def one_row(column):
        return jax.ops.segment_sum(column, flat_index, num_segments=total_cams)

    return jax.vmap(one_row)(values.reshape(width, -1))


def schur_obs(cam_jac, lm_jac, inverse, cam_values):
    applied = camera_apply(cam_jac, cam_values)
    landmark = apply_inverse(inverse, landmark_side(lm_jac, applied))
    return camera_transpose(cam_jac, applied - back_project(lm_jac, landmark))


def gather_cameras(tile):
    return lax.all_gather(tile, "dev", axis=1, tiled=True)


def reduce_cameras(terms):
    totals = lax.psum(terms, ("group", "dev"))
    width = terms.shape[1] // lax.axis_size("dev")
    return lax.dynamic_slice_in_dim(totals, lax.axis_index("dev") * width, width, 1)


def inner_product(left, right):
    return lax.psum(jnp.sum(left * right), "dev")


def body(cam_jac, lm_jac, resid, cam_index):
    total_cams = CAM_DEV * lax.axis_size("dev")
    inverse = landmark_inverse(lm_jac)
    land_rhs = apply_inverse(inverse, landmark_side(lm_jac, resid))
    errors = resid - back_project(lm_jac, land_rhs)
    stacked = jnp.concatenate(
        [camera_transpose(cam_jac, errors), jnp.sum(cam_jac * cam_jac, axis=0)], axis=0
    )
    summed = reduce_cameras(to_cameras(stacked, cam_index, total_cams))
    gradient = summed[:9]
    diagonal = summed[9:] + DAMPING
    residual = gradient
    precond = residual / diagonal
    direction = precond
    rz_now = inner_product(residual, precond)
    solution = jnp.zeros_like(gradient)
    for iteration in range(ITERS):
        whole = gather_cameras(direction)
        cam_values = jnp.take(whole, cam_index, axis=1)
        terms = to_cameras(schur_obs(cam_jac, lm_jac, inverse, cam_values), cam_index, total_cams)
        image = reduce_cameras(terms) + DAMPING * direction
        alpha = rz_now / inner_product(direction, image)
        solution = solution + alpha * direction
        residual = residual - alpha * image
        if iteration + 1 < ITERS:
            precond = residual / diagonal
            rz_next = inner_product(residual, precond)
            direction = precond + rz_next / rz_now * direction
            rz_now = rz_next
    whole_step = gather_cameras(solution)
    cam_obs = camera_apply(cam_jac, jnp.take(whole_step, cam_index, axis=1))
    landmark_step = land_rhs - apply_inverse(inverse, landmark_side(lm_jac, cam_obs))
    return (solution, residual, landmark_step)


def solution(mesh):
    in_specs = (
        P(None, None, None, ("group", "dev")),
        P(None, None, None, ("group", "dev")),
        P(None, None, ("group", "dev")),
        P(None, ("group", "dev")),
    )
    out_specs = (P(None, "dev"), P(None, "dev"), P(None, ("group", "dev")))
    return jax.shard_map(body, mesh=mesh, in_specs=in_specs, out_specs=out_specs, check_vma=False)
```

profile of v0, /device:TPU:8, one launch (start us, length us, event | category | flops | bytes accessed | tf_op | source)
XLA Modules:
  0.0 2390.0 jit_solution(14837299796872105308)
XLA Ops:
  7.2 0.0 all-reduce.5.cloned.1.call-start
  7.2 0.8 multiply_reduce_fusion.22
  8.0 0.9 multiply_reduce_fusion.13
  9.0 0.7 copy.31
  9.8 0.9 multiply_reduce_fusion.12
  10.7 0.8 sub.128
  11.5 1.0 multiply_reduce_fusion.6
  12.5 0.6 copy.28
  13.2 0.0 copy-start.2
  13.2 24.5 %scatter_custom_fusion = f32[18,8192]{0,1:T(8,128)} fusion(s32[4096]{0:T(1024)S(1)} %bitcast.43, f32[4096,18]{1,0:T(8,128)S(1)} %bitcast.38, f32[]{:T(128)} %constant.14.clone.1), kind=kCustom, calls=%fused_computation.13 | custom fusion | flops 73728 | bytes 589828 | tf_op jit(solution)/shard_map/vmap()/scatter-add | solution.py:62
  37.7 0.0 all-reduce.5.cloned.1.call-update
  37.8 0.0 all-reduce.7.cloned.1.call-start
  37.8 0.0 copy-done.2
  37.9 494.2 %all-reduce.5.cloned.1.call-done = f32[18,8192]{0,1:T(8,128)} async-done(((f32[18,8192]{0,1:T(8,128)}), f32[18,8192]{0,1:T(8,128)}) %all-reduce.5.cloned.1.call-update) | async-done | bytes 589840 | tf_op jit(solution)/shard_map/psum | solution.py:78
  532.1 1.0 fusion.7
  533.1 111.9 %all_gather.9 = f32[9,8192]{0,1:T(8,128)} all-gather(f32[9,128]{0,1:T(8,128)S(1)} %fusion.7), channel_id=1, replica_groups=mesh['group'=8,'dev'=64] {'dev'}, dimensions={1}, use_global_device_ids=true | all-gather | bytes 299520 | tf_op jit(solution)/shard_map/all_gather | solution.py:74
  645.0 16.3 gather_fusion
  661.3 1.9 select_bitcast_fusion.2
  663.3 0.6 copy.21
  663.9 0.0 copy-done
  664.1 0.6 copy.29
  664.8 24.5 %scatter_custom_fusion.1 = f32[9,8192]{0,1:T(8,128)} fusion(s32[4096]{0:T(1024)S(1)} %bitcast.44, f32[4096,9]{1,0:T(8,128)S(1)} %bitcast.40, f32[]{:T(128)} %constant.14.clone.1), kind=kCustom, calls=%fused_computation.11 | custom fusion | flops 36864 | bytes 294916 | tf_op jit(solution)/shard_map/vmap()/scatter-add | solution.py:62
  689.3 0.0 all-reduce.7.cloned.1.call-update
  689.3 0.0 all-reduce.9.cloned.1.call-start
  689.4 488.0 %all-reduce.7.cloned.1.call-done = f32[9,8192]{0,1:T(8,128)} async-done(((f32[9,8192]{0,1:T(8,128)}), f32[9,8192]{0,1:T(8,128)}) %all-reduce.7.cloned.1.call-update) | async-done | bytes 294928 | tf_op jit(solution)/shard_map/psum | solution.py:78
  1177.4 1.6 multiply_reduce_fusion.16
  1179.0 139.5 %all-reduce = (f32[]{:T(128)}, f32[]{:T(128)}) all-reduce(f32[]{:T(128)} %get-tuple-element.22, f32[]{:T(128)} %get-tuple-element.21), channel_id=1, replica_groups=mesh['group'=8,'dev'=64] {'dev'}, use_global_device_ids=true, to_apply=%region_14.0 | all-reduce | flops 2 | bytes 16 | tf_op jit(solution)/shard_map/psum | solution.py:84
  1319.8 1.6 multiply_reduce_fusion.15
  1321.4 140.7 %psum.53 = f32[]{:T(128)} all-reduce(f32[]{:T(128)} %get-tuple-element.25), channel_id=1, replica_groups=mesh['group'=8,'dev'=64] {'dev'}, use_global_device_ids=true, to_apply=%region_25.27 | all-reduce | flops 1 | bytes 8 | tf_op jit(solution)/shard_map/psum | solution.py:84
  1463.5 1.0 multiply_add_fusion.1
  1464.5 110.5 %all_gather.10 = f32[9,8192]{0,1:T(8,128)} all-gather(f32[9,128]{0,1:T(8,128)S(1)} %multiply_add_fusion.1), channel_id=1, replica_groups=mesh['group'=8,'dev'=64] {'dev'}, dimensions={1}, use_global_device_ids=true | all-gather | bytes 299520 | tf_op jit(solution)/shard_map/all_gather | solution.py:74
  1575.0 16.3 gather_fusion.1
  1591.2 1.9 select_bitcast_fusion.1
  1593.2 0.6 copy.23
  1594.0 0.6 copy.30
  1594.6 24.5 %scatter_custom_fusion.2 = f32[9,8192]{0,1:T(8,128)} fusion(s32[4096]{0:T(1024)S(1)} %bitcast.45, f32[4096,9]{1,0:T(8,128)S(1)} %bitcast.39, f32[]{:T(128)} %constant.14.clone.1), kind=kCustom, calls=%fused_computation.9 | custom fusion | flops 36864 | bytes 294916 | tf_op jit(solution)/shard_map/vmap()/scatter-add | solution.py:62
  1619.2 0.0 all-reduce.9.cloned.1.call-update
  1619.2 488.2 %all-reduce.9.cloned.1.call-done = f32[9,8192]{0,1:T(8,128)} async-done(((f32[9,8192]{0,1:T(8,128)}), f32[9,8192]{0,1:T(8,128)}) %all-reduce.9.cloned.1.call-update) | async-done | bytes 294928 | tf_op jit(solution)/shard_map/psum | solution.py:78
  2107.4 1.5 multiply_reduce_fusion.14
  2108.9 139.4 %psum.55 = f32[]{:T(128)} all-reduce(f32[]{:T(128)} %multiply_reduce_fusion.14), channel_id=1, replica_groups=mesh['group'=8,'dev'=64] {'dev'}, use_global_device_ids=true, to_apply=%region_34.36 | all-reduce | flops 1 | bytes 8 | tf_op jit(solution)/shard_map/psum | solution.py:84
  2249.7 1.0 multiply_subtract_fusion
  2250.7 0.7 copy.26
  2251.4 111.8 %all_gather.11 = f32[9,8192]{0,1:T(8,128)} all-gather(f32[9,128]{0,1:T(8,128)S(1)} %get-tuple-element.34), channel_id=1, replica_groups=mesh['group'=8,'dev'=64] {'dev'}, dimensions={1}, use_global_device_ids=true | all-gather | bytes 299520 | tf_op jit(solution)/shard_map/all_gather | solution.py:74
  2363.2 0.7 copy.27
  2363.9 16.3 gather_fusion.2
  2380.2 1.9 select_bitcast_fusion
  2382.1 0.6 copy.25
  2382.8 0.6 sub.133
  (26 shorter events, 0.5 us)
Async XLA Ops:
  7.2 524.9 %all-reduce.5.cloned.1.call-start = ((), (), s32[]{:S(2)}) async-start(), calls=%async_computation | async-start | bytes 8388608 | tf_op jit(solution)/shard_map/psum | solution.py:78
  13.2 24.6 %copy-start.2 = (s32[8,512]{1,0:T(8,128)S(1)}, s32[8,512]{1,0:T(8,128)}, u32[]{:S(2)}) copy-start(s32[8,512]{1,0:T(8,128)} %param.9) | copy-start | bytes 49156
  37.8 1139.6 %all-reduce.7.cloned.1.call-start = ((), (), s32[]{:S(2)}) async-start(), calls=%async_computation.1 | async-start | bytes 8388608 | tf_op jit(solution)/shard_map/psum | solution.py:78
  645.0 18.9 copy-start
  645.0 19.0 copy-start.1
  689.3 1418.1 %all-reduce.9.cloned.1.call-start = ((), (), s32[]{:S(2)}) async-start(), calls=%async_computation.2 | async-start | bytes 8388608 | tf_op jit(solution)/shard_map/psum | solution.py:78
Sparse Core Ops, SparseCore 0:
  37.9 494.1 all-reduce.4
  689.4 487.8 all-reduce.6
  1619.3 488.0 all-reduce.8
where the time goes:
time: 2390 us
  waiting for transfers between devices  1470 us (62%)
  blocking collectives  754 us (32%)
  other arithmetic  92.8 us (4%)
  local copies, waits for them, and re-layouts  54.8 us (2%)
    psum x3, waiting for transfers between devices, reduce_cameras(): totals = lax.psum(terms, ('group', 'dev'))  1470 us
    psum x3, blocking collectives, inner_product(): return lax.psum(jnp.sum(left * right), 'dev')  420 us
    all_gather x3, blocking collectives, gather_cameras(): return lax.all_gather(tile, 'dev', axis=1, tiled=True)  334 us
    scatter-add x3, other arithmetic, one_row(): return jax.ops.segment_sum(column, flat_index, num_segments=total_cams)  73.6 us
  transfers between devices with their start and end apart: 3, of which 3 were waited for; matrix products, arithmetic and copies ran while one was open for 0% of the time, Pallas kernels for 0%

commit v1 on v0

--- a/solution.py
+++ b/solution.py
@@ -71,7 +71,9 @@
 
 
 def gather_cameras(tile):
-    return lax.all_gather(tile, "dev", axis=1, tiled=True)
+    return jnp.concatenate(
+        lax.all_to_all(jnp.stack([tile] * lax.axis_size("dev")), "dev", 0, 0), axis=1
+    )
 
 
 def reduce_cameras(terms):

time: 2390 us -> 2090 us (0.87)
  the two profiles are of different devices: /device:TPU:8 before, /device:TPU:2 now
where the time goes in v1:
time: 2090 us
  waiting for transfers between devices  1410 us (67%)
  blocking collectives  489 us (23%)
  other arithmetic  92.2 us (4%)
  local copies, waits for them, and re-layouts  73.1 us (3%)
    psum x3, waiting for transfers between devices, reduce_cameras(): totals = lax.psum(terms, ('group', 'dev'))  1370 us
    psum x3, blocking collectives, inner_product(): return lax.psum(jnp.sum(left * right), 'dev')  426 us
    scatter-add x3, other arithmetic, one_row(): return jax.ops.segment_sum(column, flat_index, num_segments=total_cams)  73.5 us
    all_to_all x2, blocking collectives, gather_cameras(): lax.all_to_all(jnp.stack([tile] * lax.axis_size('dev')), 'dev', 0, 0)  62.4 us
  transfers between devices with their start and end apart: 4, of which 4 were waited for; matrix products, arithmetic and copies ran while one was open for 0% of the time, Pallas kernels for 0%

profile of v1, /device:TPU:2, one launch (start us, length us, event | category | flops | bytes accessed | tf_op | source)
XLA Modules:
  0.0 2089.5 jit_solution(865818515667526034)
XLA Ops:
  7.2 0.8 multiply_reduce_fusion.18
  8.0 0.9 multiply_reduce_fusion.13
  9.0 0.7 copy.55
  9.8 0.9 multiply_reduce_fusion.12
  10.7 0.8 sub.128
  11.5 1.0 multiply_reduce_fusion.6
  12.5 0.6 copy.52
  13.2 24.5 %scatter_custom_fusion = f32[18,8192]{0,1:T(8,128)} fusion(s32[4096]{0:T(1024)S(1)} %bitcast.55, f32[4096,18]{1,0:T(8,128)S(1)} %bitcast.50, f32[]{:T(128)} %constant.14.clone.1), kind=kCustom, calls=%fused_computation.13 | custom fusion | flops 73728 | bytes 589828 | tf_op jit(solution)/shard_map/vmap()/scatter-add | solution.py:62
  37.7 3.6 copy.41
  41.3 473.1 %all-reduce.5.cloned.1.call-done = f32[18,8192]{1,0:T(8,128)} async-done(((f32[18,8192]{1,0:T(8,128)}), f32[18,8192]{1,0:T(8,128)}) %all-reduce.5.cloned.1.call-update) | async-done | bytes 589840 | tf_op jit(solution)/shard_map/psum | solution.py:80
  514.4 0.8 fusion.8
  515.3 0.8 stack.27
  516.1 12.2 all-to-all-start
  528.3 0.0 all-reduce.7.cloned.1.call-start
  528.4 31.9 %all-to-all-done = f32[64,9,128]{2,1,0:T(8,128)S(1)} async-done(((f32[64,9,128]{2,1,0:T(8,128)}), f32[64,9,128]{2,1,0:T(8,128)S(1)}, u32[]{:S(2)}, u32[]{:S(2)}) %all-to-all-start) | async-done | bytes 294944 | tf_op jit(solution)/shard_map/all_to_all | solution.py:75
  560.3 2.6 copy.42
  562.9 16.3 gather_fusion
  579.2 1.9 select_bitcast_fusion.2
  581.1 0.6 copy.43
  581.8 0.3 copy-done
  582.3 0.6 copy.53
  582.9 24.5 %scatter_custom_fusion.1 = f32[9,8192]{0,1:T(8,128)} fusion(s32[4096]{0:T(1024)S(1)} %bitcast.56, f32[4096,9]{1,0:T(8,128)S(1)} %bitcast.52, f32[]{:T(128)} %constant.14.clone.1), kind=kCustom, calls=%fused_computation.11 | custom fusion | flops 36864 | bytes 294916 | tf_op jit(solution)/shard_map/vmap()/scatter-add | solution.py:62
  607.4 3.5 copy.45
  611.0 0.0 all-reduce.9.cloned.1.call-start
  611.0 450.9 %all-reduce.7.cloned.1.call-done = f32[9,8192]{1,0:T(8,128)} async-done(((f32[9,8192]{1,0:T(8,128)}), f32[9,8192]{1,0:T(8,128)}) %all-reduce.7.cloned.1.call-update) | async-done | bytes 294928 | tf_op jit(solution)/shard_map/psum | solution.py:80
  1062.0 1.5 multiply_reduce_fusion.26
  1063.4 141.3 %all-reduce = (f32[]{:T(128)}, f32[]{:T(128)}) all-reduce(f32[]{:T(128)} %get-tuple-element.22, f32[]{:T(128)} %get-tuple-element.21), channel_id=1, replica_groups=mesh['group'=8,'dev'=64] {'dev'}, use_global_device_ids=true, to_apply=%region_14.0 | all-reduce | flops 2 | bytes 16 | tf_op jit(solution)/shard_map/psum | solution.py:86
  1206.1 1.5 multiply_reduce_fusion.25
  1207.6 141.4 %psum.53 = f32[]{:T(128)} all-reduce(f32[]{:T(128)} %get-tuple-element.25), channel_id=1, replica_groups=mesh['group'=8,'dev'=64] {'dev'}, use_global_device_ids=true, to_apply=%region_25.27 | all-reduce | flops 1 | bytes 8 | tf_op jit(solution)/shard_map/psum | solution.py:86
  1350.3 0.9 multiply_add_fusion.1
  1351.2 31.6 %all_to_all.15 = f32[64,9,128]{2,1,0:T(8,128)S(1)} all-to-all(f32[64,9,128]{2,1,0:T(8,128)S(1)} %stack.28), channel_id=1, replica_groups=mesh['group'=8,'dev'=64] {'dev'}, dimensions={0} | all-to-all | bytes 589824 | tf_op jit(solution)/shard_map/all_to_all | solution.py:75
  1382.7 2.6 copy.46
  1385.4 16.3 gather_fusion.1
  1401.6 1.9 select_bitcast_fusion.1
  1403.6 0.6 copy.47
  1404.4 0.6 copy.54
  1405.0 24.5 %scatter_custom_fusion.2 = f32[9,8192]{0,1:T(8,128)} fusion(s32[4096]{0:T(1024)S(1)} %bitcast.57, f32[4096,9]{1,0:T(8,128)S(1)} %bitcast.51, f32[]{:T(128)} %constant.14.clone.1), kind=kCustom, calls=%fused_computation.9 | custom fusion | flops 36864 | bytes 294916 | tf_op jit(solution)/shard_map/vmap()/scatter-add | solution.py:62
  1429.5 3.5 copy.49
  1433.1 449.4 %all-reduce.9.cloned.1.call-done = f32[9,8192]{1,0:T(8,128)} async-done(((f32[9,8192]{1,0:T(8,128)}), f32[9,8192]{1,0:T(8,128)}) %all-reduce.9.cloned.1.call-update) | async-done | bytes 294928 | tf_op jit(solution)/shard_map/psum | solution.py:80
  1882.5 1.3 multiply_reduce_fusion.24
  1883.8 143.4 %psum.55 = f32[]{:T(128)} all-reduce(f32[]{:T(128)} %multiply_reduce_fusion.24), channel_id=1, replica_groups=mesh['group'=8,'dev'=64] {'dev'}, use_global_device_ids=true, to_apply=%region_34.36 | all-reduce | flops 1 | bytes 8 | tf_op jit(solution)/shard_map/psum | solution.py:86
  2028.5 1.4 multiply_subtract_fusion
  2030.0 30.9 %all_to_all.16 = f32[64,9,128]{2,1,0:T(8,128)S(1)} all-to-all(f32[64,9,128]{2,1,0:T(8,128)S(1)} %stack.29), channel_id=1, replica_groups=mesh['group'=8,'dev'=64] {'dev'}, dimensions={0} | all-to-all | bytes 589824 | tf_op jit(solution)/shard_map/all_to_all | solution.py:75
  2060.8 2.6 copy.50
  2063.4 16.3 gather_fusion.2
  2079.7 1.9 select_bitcast_fusion
  2081.7 0.6 copy.51
  2082.4 0.6 sub.133
  (36 shorter events, 0.7 us)
Async XLA Ops:
  7.2 507.3 %all-reduce.5.cloned.1.call-start = ((), (), s32[]{:S(2)}) async-start(), calls=%async_computation.3 | async-start | bytes 1572864 | tf_op jit(solution)/shard_map/psum | solution.py:80
  41.3 487.1 %copy-start.2 = (s32[8,512]{1,0:T(8,128)S(1)}, s32[8,512]{1,0:T(8,128)}, u32[]{:S(2)}) copy-start(s32[8,512]{1,0:T(8,128)} %param.9) | copy-start | bytes 49156
  516.1 44.2 %all-to-all-start = ((f32[64,9,128]{2,1,0:T(8,128)}), f32[64,9,128]{2,1,0:T(8,128)S(1)}, u32[]{:S(2)}, u32[]{:S(2)}) async-start(f32[64,9,128]{2,1,0:T(8,128)} %stack.27), calls=%async_computation | async-start | bytes 1048576 | tf_op jit(solution)/shard_map/all_to_all | solution.py:75
  528.3 533.6 %all-reduce.7.cloned.1.call-start = ((), (), s32[]{:S(2)}) async-start(), calls=%async_computation.4 | async-start | bytes 1048576 | tf_op jit(solution)/shard_map/psum | solution.py:80
  581.1 1.0 copy-start
  581.1 1.0 copy-start.1
  611.0 1271.5 %all-reduce.9.cloned.1.call-start = ((), (), s32[]{:S(2)}) async-start(), calls=%async_computation.5 | async-start | bytes 1048576 | tf_op jit(solution)/shard_map/psum | solution.py:80
  2029.9 33.5 %copy-start.3 = (f32[9,128]{1,0:T(8,128)}, f32[9,128]{1,0:T(8,128)S(1)}, u32[]{:S(2)}) copy-start(f32[9,128]{1,0:T(8,128)S(1)} %get-tuple-element.34) | copy-start | bytes 13828
Sparse Core Ops, SparseCore 0:
  41.4 472.9 all-reduce.4
  611.1 450.8 all-reduce.6
  1433.2 449.2 all-reduce.8
